TPU v7x, 32 devices: a whole 2x2x4 slice. The times are simulated.
32 devices in a mesh: rep: 8 (over y, x, core), ep: 4 (over z).
Axes of the slice: x: 2, y: 2, z: 4, core: 2. Of those that a mesh axis runs over, the one named last changes fastest.
Arguments:
- inputs: bfloat16 [4096, 2048], P(('rep', 'ep')), may hold values from -6 to 6
- out_grad: bfloat16 [4096, 2048], P(('rep', 'ep')), may hold values from -6 to 6
- routes: int32 [4096, 8], P(('rep', 'ep')), may hold values from 0 to 127, as said below
- gate_probs: float32 [4096, 8], P(('rep', 'ep')), may hold values from 0.05 to 0.6
- gate_weight: bfloat16 [4, 2048, 768], P('ep'), may hold values from -0.125 to 0.125
- up_weight: bfloat16 [4, 2048, 768], P('ep'), may hold values from -0.125 to 0.125
- down_weight: bfloat16 [4, 768, 2048], P('ep'), may hold values from -0.21875 to 0.21875
Outputs:
- input_grad: bfloat16 [4096, 2048], P(('rep', 'ep'))
- gate_grad: float32 [4, 2048, 768], P('ep', 'rep')
- up_grad: float32 [4, 2048, 768], P('ep', 'rep')
- down_update: float32 [4, 2048, 768], P('ep', 'rep')
Inputs may be any that keep to these rules, and one draw needn't show every extreme that they name: `routes`: each row names 8 different experts. Among the rows of one device (aligned blocks of 128 rows), each computed expert (0 to 3) is named by at most 16 rows, and in every group of devices along ep one computed expert is named by exactly 16 rows of every device of the group.
All inputs are finite; a program needn't handle non-finite values.
Results may differ from a plain program's by a relative error of at most 0.0057.
Values may be sent and summed in bfloat16 or wider, within the bound.
A program may use at most 128 MiB of HBM per device.

v0:
```python
import jax
import jax.numpy as jnp
from jax import lax
from jax.sharding import PartitionSpec as P

ITERS = 3
CAP = 16


coef_linear = 3.4445
coef_cubic = -4.775
coef_quintic = 2.0315
norm_eps = 1e-06
highest = lax.Precision.HIGHEST
rows_first = (((0,), (0,)), ((), ()))
cols_last = (((1,), (1,)), ((), ()))


def slot_tables(routes, gate_probs, owners, capacity):
    count, picks = routes.shape
    flat = routes.reshape(count * picks)
    labels = jnp.arange(owners, dtype=jnp.int32)
    onehot = (flat[:, None] == labels[None, :]).astype(jnp.int32)
    before = jnp.cumsum(onehot, axis=0) - onehot
    place = jnp.sum(before * onehot, axis=1)
    target = jnp.where(flat < owners, flat * capacity + place, -1)
    slots = jnp.arange(owners * capacity, dtype=jnp.int32)
    match = (target[None, :] == slots[:, None]).reshape(owners * capacity, count, picks)
    dispatch = jnp.sum(match.astype(jnp.float32), axis=2).astype(jnp.bfloat16)
    weight = jnp.sum(jnp.where(match, gate_probs[None, :, :], jnp.float32(0.0)), axis=(1, 2))
    return (dispatch, weight)


def gram_of(part):
    local = lax.dot_general(
        part, part, rows_first, precision=highest, preferred_element_type=jnp.float32
    )
    return lax.psum(local, "rep")


def orthogonal(summed):
    total = lax.psum(jnp.sum(summed * summed), "rep")
    current = summed / (jnp.sqrt(total) + norm_eps)
    gram = gram_of(current)
    for step in range(ITERS):
        if step > 0:
            gram = gram_of(current)
        square = jnp.dot(gram, gram, precision=highest, preferred_element_type=jnp.float32)
        poly = coef_cubic * gram + coef_quintic * square
        current = coef_linear * current + jnp.dot(
            current, poly, precision=highest, preferred_element_type=jnp.float32
        )
    return current


def per_device(inputs, out_grad, routes, gate_probs, gate_weight, up_weight, down_weight):
    owners = lax.axis_size("ep")
    groups = lax.axis_size("rep")
    width = inputs.shape[1]
    dispatch, weight = slot_tables(routes, gate_probs, owners, CAP)
    rows_send = jnp.dot(dispatch, inputs, preferred_element_type=jnp.float32).astype(jnp.bfloat16)
    grad_send = jnp.dot(dispatch, out_grad, preferred_element_type=jnp.float32) * weight[:, None]
    grad_send = grad_send.astype(jnp.bfloat16)
    rows_recv, scaled = (
        lax.all_to_all(
            rows_send.reshape(owners, CAP, width), "ep", split_axis=0, concat_axis=0, tiled=True
        ),
        lax.all_to_all(
            grad_send.reshape(owners, CAP, width), "ep", split_axis=0, concat_axis=0, tiled=True
        ),
    )
    rows_recv = rows_recv.reshape(owners * CAP, width)
    scaled = scaled.reshape(owners * CAP, width)
    w_gate = gate_weight[0]
    w_up = up_weight[0]
    w_down = down_weight[0]
    units = w_gate.shape[1]
    pre_gate = jnp.dot(rows_recv, w_gate, preferred_element_type=jnp.float32)
    pre_up = jnp.dot(rows_recv, w_up, preferred_element_type=jnp.float32)
    sigma = jax.nn.sigmoid(pre_gate)
    swish = pre_gate * sigma
    hidden = (swish * pre_up).astype(jnp.bfloat16)
    d_hidden = lax.dot_general(scaled, w_down, cols_last, preferred_element_type=jnp.float32)
    d_up = (d_hidden * swish).astype(jnp.bfloat16)
    d_gate = (d_hidden * pre_up * sigma * (1.0 + pre_gate * (1.0 - sigma))).astype(jnp.bfloat16)
    back = lax.dot_general(d_gate, w_gate, cols_last, preferred_element_type=jnp.float32)
    back = (
        back + lax.dot_general(d_up, w_up, cols_last, preferred_element_type=jnp.float32)
    ).astype(jnp.bfloat16)
    returned = lax.all_to_all(
        back.reshape(owners, CAP, width), "ep", split_axis=0, concat_axis=0, tiled=True
    ).reshape(owners * CAP, width)
    input_grad = lax.dot_general(
        dispatch, returned, rows_first, preferred_element_type=jnp.float32
    ).astype(jnp.bfloat16)
    d_both = jnp.concatenate([d_gate, d_up], axis=1)
    both = lax.dot_general(rows_recv, d_both, rows_first, preferred_element_type=jnp.float32)
    down = lax.dot_general(scaled, hidden, rows_first, preferred_element_type=jnp.float32)
    summed = lax.psum_scatter(
        jnp.concatenate([both, down], axis=1), "rep", scatter_dimension=0, tiled=True
    )
    summed = summed / groups
    gate_grad = summed[:, :units]
    up_grad = summed[:, units : 2 * units]
    down_update = orthogonal(summed[:, 2 * units :])
    return (input_grad, gate_grad[None], up_grad[None], down_update[None])


def solution(mesh):
    in_specs = (
        P(("rep", "ep"), None),
        P(("rep", "ep"), None),
        P(("rep", "ep"), None),
        P(("rep", "ep"), None),
        P("ep", None, None),
        P("ep", None, None),
        P("ep", None, None),
    )
    out_specs = (
        P(("rep", "ep"), None),
        P("ep", "rep", None),
        P("ep", "rep", None),
        P("ep", "rep", None),
    )
    return jax.shard_map(
        per_device, mesh=mesh, in_specs=in_specs, out_specs=out_specs, check_vma=False
    )
```

profile of v0, /device:TPU:0, one launch (start us, length us, event | category | flops | bytes accessed | tf_op | source)
XLA Modules:
  0.0 449.2 jit_solution(3296909406991987919)
XLA Ops:
  14.0 6.3 %all-to-all-start.1 = ((bf16[4,16,2048]{2,1,0:T(8,128)(2,1)}), bf16[4,16,2048]{2,1,0:T(8,128)(2,1)S(1)}, u32[]{:S(2)}, u32[]{:S(2)}) async-start(bf16[4,16,2048]{2,1,0:T(8,128)(2,1)} %bitcast.78), calls=%async_computation.1 | async-start | bytes 524288 | tf_op jit(solution)/shard_map/all_to_all | solution.py:65
  22.3 7.0 %all-to-all-done.1 = bf16[4,16,2048]{2,1,0:T(8,128)(2,1)S(1)} async-done(((bf16[4,16,2048]{2,1,0:T(8,128)(2,1)}), bf16[4,16,2048]{2,1,0:T(8,128)(2,1)S(1)}, u32[]{:S(2)}, u32[]{:S(2)}) %all-to-all-start.1) | async-done | bytes 262176 | tf_op jit(solution)/shard_map/all_to_all | solution.py:65
  29.3 4.0 all-to-all-start
  36.6 3.8 all-to-all-done
  40.4 2.3 fusion.53
  46.7 7.0 %pad_maximum_fusion = f32[2048,2304]{0,1:T(8,128)} fusion(f32[2048,768]{0,1:T(8,128)S(1)} %fusion.53, f32[2048,1536]{0,1:T(8,128)S(1)} %fusion.48), kind=kLoop, calls=%fused_computation | loop fusion | flops 4718592 | bytes 37748736 | tf_op jit(solution)/shard_map/concatenate | solution.py:100
  53.7 125.9 %reduce-scatter.2.cloned.1.call-done = f32[256,2304]{0,1:T(8,128)} async-done(((f32[2048,2304]{0,1:T(8,128)}), f32[256,2304]{0,1:T(8,128)}) %reduce-scatter.2.cloned.1.call-update) | async-done | bytes 2359312 | tf_op jit(solution)/shard_map/reduce_scatter | solution.py:99
  184.6 13.3 %psum.28 = f32[]{:T(128)} all-reduce(f32[]{:T(128)} %get-tuple-element.22), channel_id=1, replica_groups=mesh['rep'=8,'ep'=4] {'rep'}, use_global_device_ids=true, to_apply=%region_7.8 | all-reduce | flops 1 | bytes 8 | tf_op jit(solution)/shard_map/psum | solution.py:42
  198.6 4.9 %fusion.47 = f32[768,768]{1,0:T(8,128)} fusion(f32[256,2304]{0,1:T(8,128)} %copy-done.7, f32[]{:T(128)S(6)} %add.51), kind=kOutput, calls=%fused_computation.44 | convolution fusion | flops 1812135936 | bytes 3145732 | tf_op jit(solution)/shard_map/dot_general | solution.py:35
  203.8 62.8 %all-reduce.4.cloned.1.call-done = f32[768,768]{1,0:T(8,128)} async-done(((f32[768,768]{1,0:T(8,128)}), f32[768,768]{1,0:T(8,128)}) %all-reduce.4.cloned.1.call-update) | async-done | bytes 2359312 | tf_op jit(solution)/shard_map/psum | solution.py:38
  266.5 8.5 %fusion.70 = f32[768,768]{1,0:T(8,128)S(1)} fusion(f32[768,768]{1,0:T(8,128)} %all-reduce.4.cloned.1.call-done), kind=kOutput, calls=%fused_computation.79 | convolution fusion | flops 5435817984 | bytes 4718592 | tf_op jit(solution)/shard_map/dot_general | solution.py:48
  275.1 5.3 %fusion.29 = f32[256,768]{0,1:T(8,128)S(1)} fusion(f32[768,768]{1,0:T(8,128)S(1)} %fusion.70, f32[768,768]{1,0:T(8,128)S(1)} %copy-done.8, f32[]{:T(128)S(6)} %add.51, f32[256,2304]{0,1:T(8,128)} %copy-done.7), kind=kOutput, calls=%fused_computation.29 | convolution fusion | flops 1814495232 | bytes 7078912 | tf_op jit(solution)/shard_map/dot_general | solution.py:50
  281.3 3.5 fusion.71
  285.0 62.2 %all-reduce.6.cloned.1.call-done = f32[768,768]{1,0:T(8,128)} async-done(((f32[768,768]{1,0:T(8,128)}), f32[768,768]{1,0:T(8,128)}) %all-reduce.6.cloned.1.call-update) | async-done | bytes 2359312 | tf_op jit(solution)/shard_map/psum | solution.py:38
  347.2 8.5 %fusion.72 = f32[768,768]{1,0:T(8,128)S(1)} fusion(f32[768,768]{1,0:T(8,128)} %all-reduce.6.cloned.1.call-done), kind=kOutput, calls=%fused_computation.81 | convolution fusion | flops 5435817984 | bytes 4718592 | tf_op jit(solution)/shard_map/dot_general | solution.py:48
  355.7 3.9 fusion.32
  360.6 3.5 fusion.73
  367.3 12.6 %all_to_all.15 = bf16[4,16,2048]{2,1,0:T(8,128)(2,1)S(1)} all-to-all(bf16[4,16,2048]{2,1,0:T(8,128)(2,1)S(1)} %bitcast.81), channel_id=1, replica_groups=mesh['rep'=8,'ep'=4] {'ep'}, dimensions={0} | all-to-all | bytes 524288 | tf_op jit(solution)/shard_map/all_to_all | solution.py:90
  381.0 2.3 copy.51
  383.3 2.3 copy.52
  385.6 40.9 %all-reduce.8.cloned.1.call-done = f32[768,768]{1,0:T(8,128)} async-done(((f32[768,768]{1,0:T(8,128)}), f32[768,768]{1,0:T(8,128)}) %all-reduce.8.cloned.1.call-update) | async-done | bytes 2359312 | tf_op jit(solution)/shard_map/psum | solution.py:38
  426.6 8.5 %fusion.74 = f32[768,768]{1,0:T(8,128)S(1)} fusion(f32[768,768]{1,0:T(8,128)} %all-reduce.8.cloned.1.call-done), kind=kOutput, calls=%fused_computation.83 | convolution fusion | flops 5435817984 | bytes 4718592 | tf_op jit(solution)/shard_map/dot_general | solution.py:48
  435.1 4.8 %fusion.38 = f32[1,256,768]{1,2,0:T(8,128)} fusion(f32[256,768]{0,1:T(8,128)S(1)} %copy-done.4, f32[768,768]{1,0:T(8,128)S(1)} %fusion.74, f32[768,768]{1,0:T(8,128)S(1)} %copy-done.1), kind=kOutput, calls=%fused_computation.32 | convolution fusion | flops 1814102016 | bytes 6291456 | tf_op jit(solution)/shard_map/dot_general | solution.py:50
  439.9 2.3 copy.53
  (64 shorter events, 27.8 us)
Async XLA Ops:
  7.2 26.2 %copy-start = (bf16[1,2048,768]{2,1,0:T(8,128)(2,1)S(1)}, bf16[1,2048,768]{2,1,0:T(8,128)(2,1)}, u32[]{:S(2)}) copy-start(bf16[1,2048,768]{2,1,0:T(8,128)(2,1)} %param.11) | copy-start | bytes 9437188
  14.0 15.2 %all-to-all-start.1 = ((bf16[4,16,2048]{2,1,0:T(8,128)(2,1)}), bf16[4,16,2048]{2,1,0:T(8,128)(2,1)S(1)}, u32[]{:S(2)}, u32[]{:S(2)}) async-start(bf16[4,16,2048]{2,1,0:T(8,128)(2,1)} %bitcast.78), calls=%async_computation.1 | async-start | bytes 524288 | tf_op jit(solution)/shard_map/all_to_all | solution.py:65
  29.3 11.1 %all-to-all-start = ((bf16[4,16,2048]{2,1,0:T(8,128)(2,1)}), bf16[4,16,2048]{2,1,0:T(8,128)(2,1)}, u32[]{:S(2)}, u32[]{:S(2)}) async-start(bf16[4,16,2048]{2,1,0:T(8,128)(2,1)} %bitcast.80), calls=%async_computation | async-start | bytes 524288 | tf_op jit(solution)/shard_map/all_to_all | solution.py:68
  33.3 146.2 %reduce-scatter.2.cloned.1.call-start = ((), (), s32[]{:S(2)}) async-start(), calls=%async_computation.4 | async-start | bytes 21233664 | tf_op jit(solution)/shard_map/reduce_scatter | solution.py:99
  33.4 2.0 copy-start.5
  40.4 2.3 copy-start.11
  40.4 2.3 copy-start.12
  40.4 2.3 copy-start.13
  44.8 1.9 copy-start.14
  53.6 212.9 %all-reduce.4.cloned.1.call-start = ((), (), s32[]{:S(2)}) async-start(), calls=%async_computation.5 | async-start | bytes 4718592 | tf_op jit(solution)/shard_map/psum | solution.py:38
  181.4 1.4 copy-start.7
  203.6 143.6 %all-reduce.6.cloned.1.call-start = ((), (), s32[]{:S(2)}) async-start(), calls=%async_computation.6 | async-start | bytes 4718592 | tf_op jit(solution)/shard_map/psum | solution.py:38
  266.5 8.5 %copy-start.8 = (f32[768,768]{1,0:T(8,128)S(1)}, f32[768,768]{1,0:T(8,128)}, u32[]{:S(2)}) copy-start(f32[768,768]{1,0:T(8,128)} %all-reduce.4.cloned.1.call-done) | copy-start | bytes 7077892
  280.4 0.9 copy-start.9
  284.8 141.8 %all-reduce.8.cloned.1.call-start = ((), (), s32[]{:S(2)}) async-start(), calls=%async_computation.7 | async-start | bytes 4718592 | tf_op jit(solution)/shard_map/psum | solution.py:38
  347.2 8.5 %copy-start.2 = (f32[768,768]{1,0:T(8,128)S(1)}, f32[768,768]{1,0:T(8,128)}, u32[]{:S(2)}) copy-start(f32[768,768]{1,0:T(8,128)} %all-reduce.6.cloned.1.call-done) | copy-start | bytes 7077892
  347.2 8.5 %copy-start.10 = (f32[256,768]{0,1:T(8,128)S(1)}, f32[256,768]{0,1:T(8,128)}, u32[]{:S(2)}) copy-start(f32[256,768]{0,1:T(8,128)} %copy-done.9) | copy-start | bytes 2359300
  359.7 0.9 copy-start.3
  360.6 3.5 copy-start.15
  364.1 1.9 copy-start.6
  426.6 8.5 %copy-start.1 = (f32[768,768]{1,0:T(8,128)S(1)}, f32[768,768]{1,0:T(8,128)}, u32[]{:S(2)}) copy-start(f32[768,768]{1,0:T(8,128)} %all-reduce.8.cloned.1.call-done) | copy-start | bytes 7077892
  426.6 8.5 %copy-start.4 = (f32[256,768]{0,1:T(8,128)S(1)}, f32[256,768]{0,1:T(8,128)}, u32[]{:S(2)}) copy-start(f32[256,768]{0,1:T(8,128)} %copy-done.3) | copy-start | bytes 2359300
Sparse Core Ops, SparseCore 0:
  53.8 125.7 reduce-scatter.1
  203.7 62.8 all-reduce.3
  284.9 62.2 all-reduce.5
  364.2 62.3 all-reduce.7
where the time goes:
time: 456 us; the launch traced here: 449 us
  waiting for transfers between devices  302 us (66%)
  matrix products  67.7 us (15%)
  blocking collectives  25.9 us (6%)
  between operations  15.2 us (3%)
  other arithmetic  14 us (3%)
  local copies, waits for them, and re-layouts  13 us (3%)
  starting transfers between devices  10.9 us (2%)
    psum x3, waiting for transfers between devices, gram_of(): return lax.psum(local, 'rep')  166 us
    reduce_scatter x1, waiting for transfers between devices, per_device(): lax.psum_scatter(jnp.concatenate([both, down], axis=1), 'rep', scatter_di...  126 us
    dot_general x3, matrix products, orthogonal(): jnp.dot(gram, gram, precision=highest, preferred_element_type=jnp.float32)  25.5 us
    dot_general x3, matrix products, orthogonal(): jnp.dot(current, poly, precision=highest, preferred_element_type=jnp.floa...  14.1 us
    psum x1, blocking collectives, orthogonal(): total = lax.psum(jnp.sum(summed * summed), 'rep')  13.3 us
    all_to_all x1, blocking collectives, per_device(): lax.all_to_all(back.reshape(owners, CAP, width), 'ep', split_axis=0, conc...  12.6 us
    unnamed x36, local copies, waits for them, and re-layouts  12.5 us
    dot_general x3, matrix products, gram_of(): lax.dot_general(part, part, rows_first, precision=highest, preferred_elem...  11.8 us
  transfers between devices with their start and end apart: 6, of which 6 were waited for; matrix products, arithmetic and copies ran while one was open for 3% of the time, Pallas kernels for 0%

commit v1 on v0

--- a/solution.py
+++ b/solution.py
@@ -11,7 +11,6 @@
 coef_cubic = -4.775
 coef_quintic = 2.0315
 norm_eps = 1e-06
-highest = lax.Precision.HIGHEST
 rows_first = (((0,), (0,)), ((), ()))
 cols_last = (((1,), (1,)), ((), ()))
 
@@ -31,26 +30,49 @@
     return (dispatch, weight)
 
 
-def gram_of(part):
-    local = lax.dot_general(
-        part, part, rows_first, precision=highest, preferred_element_type=jnp.float32
-    )
-    return lax.psum(local, "rep")
+high = lax.Precision.HIGH
 
 
-def orthogonal(summed):
-    total = lax.psum(jnp.sum(summed * summed), "rep")
-    current = summed / (jnp.sqrt(total) + norm_eps)
-    gram = gram_of(current)
+def mul(left, right):
+    return jnp.dot(left, right, precision=high, preferred_element_type=jnp.float32)
+
+
+def factor(power, identity):
+    return coef_linear * identity + coef_cubic * power + coef_quintic * mul(power, power)
+
+
+def small_rows(rows_own, rows_all, hidden, groups):
+    outer = lax.dot_general(rows_all, rows_all, cols_last, preferred_element_type=jnp.float32)
+    hid = lax.dot_general(hidden, hidden, cols_last, preferred_element_type=jnp.float32)
+    total = jnp.maximum(jnp.sum(outer * hid), 0.0) / (groups * groups)
+    scale = 1.0 / (groups * (jnp.sqrt(total) + norm_eps))
+    power = mul(hid * scale, outer * scale)
+    identity = jnp.eye(power.shape[0], dtype=jnp.float32)
+    left = rows_own.astype(jnp.float32).T * scale
     for step in range(ITERS):
-        if step > 0:
-            gram = gram_of(current)
-        square = jnp.dot(gram, gram, precision=highest, preferred_element_type=jnp.float32)
-        poly = coef_cubic * gram + coef_quintic * square
-        current = coef_linear * current + jnp.dot(
-            current, poly, precision=highest, preferred_element_type=jnp.float32
-        )
-    return current
+        step_factor = factor(power, identity)
+        left = mul(left, step_factor)
+        if step < ITERS - 1:
+            power = mul(mul(power, step_factor), step_factor)
+    return mul(left, hidden.astype(jnp.float32))
+
+
+def small_units(rows_own, rows_all, hidden, groups):
+    whole = lax.dot_general(rows_all, hidden, rows_first, preferred_element_type=jnp.float32) / groups
+    own = lax.dot_general(rows_own, hidden, rows_first, preferred_element_type=jnp.float32) / groups
+    norm = jnp.sqrt(jnp.sum(whole * whole)) + norm_eps
+    whole = whole / norm
+    own = own / norm
+    power = lax.dot_general(
+        whole, whole, rows_first, precision=high, preferred_element_type=jnp.float32
+    )
+    identity = jnp.eye(power.shape[0], dtype=jnp.float32)
+    for step in range(ITERS):
+        step_factor = factor(power, identity)
+        own = mul(own, step_factor)
+        if step < ITERS - 1:
+            power = mul(mul(power, step_factor), step_factor)
+    return own
 
 
 def per_device(inputs, out_grad, routes, gate_probs, gate_weight, up_weight, down_weight):
@@ -61,16 +83,18 @@
     rows_send = jnp.dot(dispatch, inputs, preferred_element_type=jnp.float32).astype(jnp.bfloat16)
     grad_send = jnp.dot(dispatch, out_grad, preferred_element_type=jnp.float32) * weight[:, None]
     grad_send = grad_send.astype(jnp.bfloat16)
-    rows_recv, scaled = (
-        lax.all_to_all(
-            rows_send.reshape(owners, CAP, width), "ep", split_axis=0, concat_axis=0, tiled=True
-        ),
-        lax.all_to_all(
-            grad_send.reshape(owners, CAP, width), "ep", split_axis=0, concat_axis=0, tiled=True
-        ),
-    )
-    rows_recv = rows_recv.reshape(owners * CAP, width)
-    scaled = scaled.reshape(owners * CAP, width)
+    rows = owners * CAP
+    both_send = jnp.concatenate([rows_send, grad_send], axis=1)
+    both_recv = lax.all_to_all(
+        both_send.reshape(owners, CAP, 2 * width), "ep", split_axis=0, concat_axis=0, tiled=True
+    ).reshape(rows, 2 * width)
+    rows_recv = both_recv[:, :width]
+    scaled = both_recv[:, width:]
+    scaled_all = lax.all_gather(scaled, "rep", axis=0, tiled=True)
+    rows_own = lax.all_to_all(
+        rows_recv.reshape(rows, groups, width // groups).transpose(1, 0, 2),
+        "rep", split_axis=0, concat_axis=0, tiled=True,
+    ).reshape(groups * rows, width // groups)
     w_gate = gate_weight[0]
     w_up = up_weight[0]
     w_down = down_weight[0]
@@ -93,16 +117,19 @@
     input_grad = lax.dot_general(
         dispatch, returned, rows_first, preferred_element_type=jnp.float32
     ).astype(jnp.bfloat16)
-    d_both = jnp.concatenate([d_gate, d_up], axis=1)
-    both = lax.dot_general(rows_recv, d_both, rows_first, preferred_element_type=jnp.float32)
-    down = lax.dot_general(scaled, hidden, rows_first, preferred_element_type=jnp.float32)
-    summed = lax.psum_scatter(
-        jnp.concatenate([both, down], axis=1), "rep", scatter_dimension=0, tiled=True
+    units_all = lax.all_gather(
+        jnp.concatenate([d_gate, d_up, hidden], axis=1), "rep", axis=0, tiled=True
     )
-    summed = summed / groups
-    gate_grad = summed[:, :units]
-    up_grad = summed[:, units : 2 * units]
-    down_update = orthogonal(summed[:, 2 * units :])
+    both = lax.dot_general(
+        rows_own, units_all[:, : 2 * units], rows_first, preferred_element_type=jnp.float32
+    ) / groups
+    gate_grad = both[:, :units]
+    up_grad = both[:, units:]
+    hidden_all = units_all[:, 2 * units :]
+    share = width // groups
+    scaled_own = lax.dynamic_slice_in_dim(scaled_all, lax.axis_index("rep") * share, share, axis=1)
+    form = small_rows if groups * rows < units else small_units
+    down_update = form(scaled_own, scaled_all, hidden_all, groups)
     return (input_grad, gate_grad[None], up_grad[None], down_update[None])
 
 

time: 456 us -> 135 us (0.30); the launches traced: 449 us -> 135 us
  waiting for transfers between devices: 302 us -> 41.3 us
  matrix products: 67.7 us -> 38.2 us
  other arithmetic: 14 us -> 4.43 us
  local copies, waits for them, and re-layouts: 13 us -> 7.02 us
  blocking collectives: 25.9 us -> 20.9 us
    psum x3 -> x0, waiting for transfers between devices: 166 us -> none  [gram_of(): return lax.psum(local, 'rep')]
    reduce_scatter x1 -> x0, waiting for transfers between devices: 126 us -> none  [per_device(): lax.psum_scatter(jnp.concatenate([both, down], axis=1), 'rep', scatter_di...]
    all_gather x0 -> x2, waiting for transfers between devices: none -> 34.8 us  [the longest x1 28.7 us: per_device(): scaled_all = lax.all_gather(scaled, 'rep', axis=0, tiled=True)]
    dot_general x11 -> x15, matrix products: 55.6 us -> 27.5 us  [the longest x12 16.9 us: mul(): jnp.dot(left, right, precision=high, preferred_element_type=jnp.float32)]
    psum x1 -> x0, blocking collectives: 13.3 us -> none  [orthogonal(): total = lax.psum(jnp.sum(summed * summed), 'rep')]
    unnamed x36 -> x14, local copies, waits for them, and re-layouts: 12.5 us -> 2.62 us
    all_to_all x1, blocking collectives: 12.6 us -> 20.9 us  [per_device(): lax.all_to_all(both_send.reshape(owners, CAP, 2 * width), 'ep', split_axi...]
    concatenate x1 -> x2, other arithmetic: 6.96 us -> 0.77 us  [the longest x1 0.73 us: per_device(): jnp.concatenate([d_gate, d_up, hidden], axis=1)]
  transfers between devices with their start and end apart: 6 -> 4, of which waited for: 6 -> 3; matrix products, arithmetic and copies ran while one was open for 3% -> 24% of each run, Pallas kernels for 0% -> 0%
where the time goes in v1:
time: 135 us
  waiting for transfers between devices  41.3 us (31%)
  matrix products  38.2 us (28%)
  blocking collectives  20.9 us (15%)
  between operations  15 us (11%)
  starting transfers between devices  7.71 us (6%)
  local copies, waits for them, and re-layouts  7.02 us (5%)
  other arithmetic  4.43 us (3%)
    all_gather x1, waiting for transfers between devices, per_device(): scaled_all = lax.all_gather(scaled, 'rep', axis=0, tiled=True)  28.7 us
    all_to_all x1, blocking collectives, per_device(): lax.all_to_all(both_send.reshape(owners, CAP, 2 * width), 'ep', split_axi...  20.9 us
    dot_general x12, matrix products, mul(): jnp.dot(left, right, precision=high, preferred_element_type=jnp.float32)  16.9 us
    all_to_all x1, waiting for transfers between devices, per_device(): lax.all_to_all(back.reshape(owners, CAP, width), 'ep', split_axis=0, conc...  6.38 us
    all_gather x1, waiting for transfers between devices, per_device(): lax.all_gather(jnp.concatenate([d_gate, d_up, hidden], axis=1), 'rep', ax...  6.1 us
    dot_general x1, matrix products, small_rows(): lax.dot_general(rows_all, rows_all, cols_last, preferred_element_type=jnp...  5.38 us
    all_to_all x1, starting transfers between devices, per_device(): lax.all_to_all(rows_recv.reshape(rows, groups, width // groups).transpose...  4.23 us
    all_to_all x1, starting transfers between devices, per_device(): lax.all_to_all(back.reshape(owners, CAP, width), 'ep', split_axis=0, conc...  3.41 us
  transfers between devices with their start and end apart: 4, of which 3 were waited for; matrix products, arithmetic and copies ran while one was open for 24% of the time, Pallas kernels for 0%

profile of v1, /device:TPU:0, one launch (start us, length us, event | category | flops | bytes accessed | tf_op | source)
XLA Modules:
  0.0 134.5 jit_solution(9191875859332855497)
XLA Ops:
  8.4 1.1 reduce-window.6
  11.0 1.4 %convert_reduce_fusion = (bf16[64,128]{1,0:T(8,128)(2,1)S(1)}, f32[64]{0:T(128)S(1)}) fusion(s32[128,8]{0,1:T(8,128)S(1)} %add_select_fusion, f32[128,8]{0,1:T(8,128)} %param.10), kind=kLoop, calls=%fused_computation.47 | loop fusion | flops 319424 | bytes 24832 | tf_op jit(solution)/shard_map/reduce_sum | solution.py:28
  12.4 1.3 convolution_convert_fusion.1
  13.6 1.3 fusion.13
  15.0 20.9 %all_to_all.15 = bf16[4,16,4096]{2,1,0:T(8,128)(2,1)S(1)} all-to-all(bf16[4,16,4096]{2,1,0:T(8,128)(2,1)S(1)} %bitcast.88), channel_id=1, replica_groups=mesh['rep'=8,'ep'=4] {'ep'}, dimensions={0} | all-to-all | bytes 1048576 | tf_op jit(solution)/shard_map/all_to_all | solution.py:88
  36.5 1.1 fusion.8
  39.1 1.9 %fusion.45 = (bf16[64,2048]{1,0:T(8,128)(2,1)}, bf16[64,2048]{1,0:T(8,128)(2,1)}) fusion(bf16[64,4096]{1,0:T(8,128)(2,1)} %bitcast.87), kind=kLoop, calls=%fused_computation.71 | loop fusion | bytes 1048576 | tf_op jit(solution)/shard_map/slice | solution.py:92
  41.0 2.9 %fusion = f32[64,2048]{1,0:T(8,128)S(1)} fusion(bf16[64,768]{1,0:T(8,128)(2,1)S(1)} %get-tuple-element.11, bf16[1,2048,768]{2,1,0:T(8,128)(2,1)} %param.11), kind=kOutput, calls=%fused_computation | convolution fusion | flops 201326592 | bytes 3768320 | tf_op jit(solution)/shard_map/dot_general | solution.py:110
  43.9 1.8 %fusion.14 = bf16[64,2048]{1,0:T(8,128)(2,1)} fusion(f32[64,2048]{1,0:T(8,128)S(1)} %fusion, bf16[64,768]{1,0:T(8,128)(2,1)S(1)} %get-tuple-element.12, bf16[1,2048,768]{2,1,0:T(8,128)(2,1)S(1)} %copy-done), kind=kOutput, calls=%fused_computation.15 | convolution fusion | flops 201588736 | bytes 4030464 | tf_op jit(solution)/shard_map/dot_general | solution.py:112
  45.7 3.4 %all-to-all-start.1 = ((bf16[4,16,2048]{2,1,0:T(8,128)(2,1)}), bf16[4,16,2048]{2,1,0:T(8,128)(2,1)S(1)}, u32[]{:S(2)}, u32[]{:S(2)}) async-start(bf16[4,16,2048]{2,1,0:T(8,128)(2,1)} %bitcast.92), calls=%async_computation.1 | async-start | bytes 524288 | tf_op jit(solution)/shard_map/all_to_all | solution.py:114
  50.9 6.4 %all-to-all-done.1 = bf16[4,16,2048]{2,1,0:T(8,128)(2,1)S(1)} async-done(((bf16[4,16,2048]{2,1,0:T(8,128)(2,1)}), bf16[4,16,2048]{2,1,0:T(8,128)(2,1)S(1)}, u32[]{:S(2)}, u32[]{:S(2)}) %all-to-all-start.1) | async-done | bytes 262176 | tf_op jit(solution)/shard_map/all_to_all | solution.py:114
  57.3 4.2 %all-to-all-start.2 = ((bf16[8,64,256]{2,1,0:T(8,128)(2,1)}), bf16[8,64,256]{2,1,0:T(8,128)(2,1)}, u32[]{:S(2)}, u32[]{:S(2)}) async-start(bf16[8,64,256]{2,1,0:T(8,128)(2,1)} %copy.47), calls=%async_computation.2 | async-start | bytes 524288 | tf_op jit(solution)/shard_map/all_to_all | solution.py:94
  61.5 1.1 convolution_convert_fusion
  62.6 6.1 %all-gather.3.cloned.1.call-done = bf16[512,2304]{1,0:T(8,128)(2,1)} async-done(((bf16[64,2304]{1,0:T(8,128)(2,1)}), bf16[512,2304]{1,0:T(8,128)(2,1)}) %all-gather.3.cloned.1.call-update) | async-done | bytes 2359312 | tf_op jit(solution)/shard_map/all_gather | solution.py:120
  68.7 3.0 %fusion.25 = f32[512,512]{1,0:T(8,128)} fusion(bf16[512,2304]{1,0:T(8,128)(2,1)} %all-gather.3.cloned.1.call-done), kind=kOutput, calls=%fused_computation.36 | convolution fusion | flops 402653184 | bytes 1835008 | tf_op jit(solution)/shard_map/dot_general | solution.py:46
  71.8 28.7 %all-gather.5.cloned.1.call-done = bf16[512,2048]{1,0:T(8,128)(2,1)} async-done(((bf16[64,2048]{1,0:T(8,128)(2,1)}), bf16[512,2048]{1,0:T(8,128)(2,1)}) %all-gather.5.cloned.1.call-update) | async-done | bytes 2097168 | tf_op jit(solution)/shard_map/all_gather | solution.py:93
  100.5 5.4 %multiply_reduce_fusion = (f32[]{:T(128)}, f32[512,512]{1,0:T(8,128)}) fusion(f32[512,512]{1,0:T(8,128)} %fusion.25, bf16[512,2048]{1,0:T(8,128)(2,1)} %all-gather.5.cloned.1.call-done), kind=kOutput, calls=%fused_computation.32 | convolution fusion | flops 1074266112 | bytes 4194308 | tf_op jit(solution)/shard_map/dot_general | solution.py:45
  106.6 2.6 %fusion.21 = f32[512,512]{1,0:T(8,128)S(1)} fusion(f32[512,512]{1,0:T(8,128)} %get-tuple-element.14, f32[512,512]{1,0:T(8,128)} %fusion.25, f32[]{:T(128)S(6)} %div.19), kind=kOutput, calls=%fused_computation.28 | convolution fusion | flops 805830656 | bytes 3145732 | tf_op jit(solution)/shard_map/dot_general | solution.py:37
  115.4 2.0 %fusion.18 = f32[512,512]{1,0:T(8,128)} fusion(f32[512,512]{1,0:T(8,128)S(1)} %fusion.50), kind=kOutput, calls=%fused_computation.22 | convolution fusion | flops 806879232 | bytes 2097152 | tf_op jit(solution)/shard_map/dot_general | solution.py:37
  117.4 1.6 %fusion.28 = f32[256,512]{1,0:T(8,128)S(1)} fusion(f32[512,512]{1,0:T(8,128)S(1)} %fusion.20, f32[]{:T(128)S(6)} %div.19, bf16[512,2048]{1,0:T(8,128)(2,1)} %all-gather.5.cloned.1.call-done, s32[]{:T(128)S(6)} %select_n.17), kind=kOutput, calls=%fused_computation.40 | convolution fusion | flops 402915328 | bytes 1835016 | tf_op jit(solution)/shard_map/dot_general | solution.py:37
  119.0 1.4 %fusion.48 = f32[256,512]{1,0:T(8,128)} fusion(f32[256,512]{1,0:T(8,128)S(1)} %fusion.28, f32[512,512]{1,0:T(8,128)S(1)} %fusion.19), kind=kOutput, calls=%fused_computation.74 | convolution fusion | flops 402653184 | bytes 2097152 | tf_op jit(solution)/shard_map/dot_general | solution.py:37
  120.4 2.1 %convolution_multiply_fusion = f32[256,1536]{1,0:T(8,128)S(1)} fusion(bf16[512,256]{1,0:T(8,128)(2,1)} %bitcast.9, bf16[512,2304]{1,0:T(8,128)(2,1)} %all-gather.3.cloned.1.call-done), kind=kOutput, calls=%fused_computation.10 | convolution fusion | flops 403046400 | bytes 3407872 | tf_op jit(solution)/shard_map/dot_general | solution.py:123
  122.5 1.3 slice_bitcast_fusion
  125.1 2.6 %convolution_bitcast_fusion = f32[1,256,768]{2,1,0:T(8,128)} fusion(f32[256,512]{1,0:T(8,128)S(1)} %fusion.51, bf16[512,2304]{1,0:T(8,128)(2,1)} %all-gather.3.cloned.1.call-done), kind=kOutput, calls=%fused_computation.27 | convolution fusion | flops 603979776 | bytes 2097152 | tf_op jit(solution)/shard_map/dot_general | solution.py:37
  (41 shorter events, 14.0 us)
Async XLA Ops:
  7.2 30.4 %copy-start = (bf16[1,2048,768]{2,1,0:T(8,128)(2,1)S(1)}, bf16[1,2048,768]{2,1,0:T(8,128)(2,1)}, u32[]{:S(2)}) copy-start(bf16[1,2048,768]{2,1,0:T(8,128)(2,1)} %param.12) | copy-start | bytes 9437188
  7.2 61.5 %all-gather.3.cloned.1.call-start = ((), (), s32[]{:S(2)}) async-start(), calls=%async_computation.3 | async-start | bytes 2654208 | tf_op jit(solution)/shard_map/all_gather | solution.py:120
  10.2 25.7 %copy-start.1 = (bf16[1,2048,768]{2,1,0:T(8,128)(2,1)S(1)}, bf16[1,2048,768]{2,1,0:T(8,128)(2,1)}, u32[]{:S(2)}) copy-start(bf16[1,2048,768]{2,1,0:T(8,128)(2,1)} %param.11) | copy-start | bytes 9437188
  15.0 21.5 %copy-start.4 = (bf16[1,768,2048]{2,1,0:T(8,128)(2,1)S(1)}, bf16[1,768,2048]{2,1,0:T(8,128)(2,1)}, u32[]{:S(2)}) copy-start(bf16[1,768,2048]{2,1,0:T(8,128)(2,1)} %param.13) | copy-start | bytes 9437188
  35.8 1.7 %copy-start.2 = (bf16[4,16,4096]{2,1,0:T(8,128)(2,1)}, bf16[4,16,4096]{2,1,0:T(8,128)(2,1)S(1)}, u32[]{:S(2)}) copy-start(bf16[4,16,4096]{2,1,0:T(8,128)(2,1)S(1)} %all_to_all.15) | copy-start | bytes 1572868
  39.0 61.5 %all-gather.5.cloned.1.call-start = ((), (), s32[]{:S(2)}) async-start(), calls=%async_computation.4 | async-start | bytes 2359296 | tf_op jit(solution)/shard_map/all_gather | solution.py:93
  45.7 11.6 %all-to-all-start.1 = ((bf16[4,16,2048]{2,1,0:T(8,128)(2,1)}), bf16[4,16,2048]{2,1,0:T(8,128)(2,1)S(1)}, u32[]{:S(2)}, u32[]{:S(2)}) async-start(bf16[4,16,2048]{2,1,0:T(8,128)(2,1)} %bitcast.92), calls=%async_computation.1 | async-start | bytes 524288 | tf_op jit(solution)/shard_map/all_to_all | solution.py:114
  57.3 63.2 %all-to-all-start.2 = ((bf16[8,64,256]{2,1,0:T(8,128)(2,1)}), bf16[8,64,256]{2,1,0:T(8,128)(2,1)}, u32[]{:S(2)}, u32[]{:S(2)}) async-start(bf16[8,64,256]{2,1,0:T(8,128)(2,1)} %copy.47), calls=%async_computation.2 | async-start | bytes 524288 | tf_op jit(solution)/shard_map/all_to_all | solution.py:94
  122.5 1.6 %copy-start.3 = (f32[512,512]{1,0:T(8,128)S(1)}, f32[512,512]{1,0:T(8,128)}, u32[]{:S(2)}) copy-start(f32[512,512]{1,0:T(8,128)} %fusion.18) | copy-start | bytes 3145732
  122.5 1.9 %copy-start.5 = (f32[256,512]{1,0:T(8,128)S(1)}, f32[256,512]{1,0:T(8,128)}, u32[]{:S(2)}) copy-start(f32[256,512]{1,0:T(8,128)} %fusion.48) | copy-start | bytes 1572868
Sparse Core Ops, SparseCore 0:
  39.2 29.5 all-gather.2
  71.2 29.2 all-gather.4

commit v2 on v1

--- a/solution.py
+++ b/solution.py
@@ -1,6 +1,10 @@
+import functools
+
 import jax
 import jax.numpy as jnp
 from jax import lax
+from jax.experimental import pallas as pl
+from jax.experimental.pallas import tpu as pltpu
 from jax.sharding import PartitionSpec as P
 
 ITERS = 3
@@ -75,15 +79,240 @@
     return own
 
 
+rows_cols = (((1,), (0,)), ((), ()))
+
+
+def dot(left, right, dims=rows_cols):
+    return lax.dot_general(left, right, dims, preferred_element_type=jnp.float32)
+
+
+def split(value):
+    top = value.astype(jnp.bfloat16)
+    return top, (value - top.astype(jnp.float32)).astype(jnp.bfloat16)
+
+
+def dot3(left, right):
+    return dot(left[0], right[0]) + (dot(left[0], right[1]) + dot(left[1], right[0]))
+
+
+def remote(src, dst, send, recv, device):
+    return pltpu.make_async_remote_copy(
+        src_ref=src, dst_ref=dst, send_sem=send, recv_sem=recv,
+        device_id=device, device_id_type=pl.DeviceIdType.MESH,
+    )
+
+
+def kernel(
+    owners, groups,
+    inputs, out_grad, routes, gate_probs, gate_hbm, up_hbm, down_hbm,
+    input_grad, gate_grad, up_grad, down_update,
+    w_gate, w_up, w_down, x_send, g_send, x_recv, s_all, h_all, d_all, x_own, back_send, ret,
+    w_sem, xs_sem, xr_sem, gs_sem, gr_sem, bs_sem, br_sem,
+    os_sem, or_sem, ss_sem, sr_sem, hs_sem, hr_sem, ds_sem, dr_sem,
+):
+    me = lax.axis_index("ep")
+    rep = lax.axis_index("rep")
+    core = rep % 2
+    chip = rep // 2
+    chips = groups // 2
+    sibling = chip * 2 + (1 - core)
+    tokens, width = inputs.shape
+    units = h_all.shape[2]
+    rows = owners * CAP
+    share = width // groups
+    near = [(me + k) % owners for k in range(1, owners)]
+    far = [((chip + k) % chips) * 2 + core for k in range(1, chips)]
+    others = [(rep + k) % groups for k in range(1, groups)]
+
+    loads = [
+        pltpu.make_async_copy(src, dst, w_sem.at[n])
+        for n, (src, dst) in enumerate(((gate_hbm.at[0], w_gate), (up_hbm.at[0], w_up), (down_hbm.at[0], w_down)))
+    ]
+    for load in loads:
+        load.start()
+    barrier = pltpu.get_barrier_semaphore()
+    for peer in near:
+        pl.semaphore_signal(barrier, inc=1, device_id={"ep": peer}, device_id_type=pl.DeviceIdType.MESH)
+    for peer in others:
+        pl.semaphore_signal(barrier, inc=1, device_id={"rep": peer}, device_id_type=pl.DeviceIdType.MESH)
+
+    lane = lax.broadcasted_iota(jnp.int32, (tokens, 128), 1)
+    place = (lane % CAP).astype(jnp.float32)
+    expert = jnp.where(lane < rows, lane // CAP, -1)
+    named = jnp.zeros((tokens, 128), jnp.float32)
+    weight = jnp.zeros((tokens, 128), jnp.float32)
+    for k in range(routes.shape[1]):
+        hit = routes[:, k : k + 1] == expert
+        named = named + jnp.where(hit, 1.0, 0.0)
+        weight = weight + jnp.where(hit, gate_probs[:, k : k + 1], 0.0)
+    earlier = lax.broadcasted_iota(jnp.int32, (tokens, tokens), 1) < lax.broadcasted_iota(
+        jnp.int32, (tokens, tokens), 0
+    )
+    before = dot(jnp.where(earlier, 1.0, 0.0).astype(jnp.bfloat16), named.astype(jnp.bfloat16))
+    slots = jnp.where(before == place, named, 0.0)
+    dispatch = slots.T[:rows].astype(jnp.bfloat16)
+    weight = jnp.sum((slots * weight).T[:rows], axis=1, keepdims=True)
+    x_send[...] = dot(dispatch, inputs[...]).astype(jnp.bfloat16).reshape(owners, CAP, width)
+    pl.semaphore_wait(barrier, len(near) + len(others))
+    sends = []
+
+    def send(*spec):
+        copy = remote(*spec)
+        copy.start()
+        sends.append(copy)
+
+    for n, peer in enumerate(near):
+        send(x_send.at[peer], x_recv.at[me], xs_sem.at[n], xr_sem.at[me], {"ep": peer})
+    g_send[...] = (dot(dispatch, out_grad[...]) * weight).astype(jnp.bfloat16).reshape(owners, CAP, width)
+    for n, peer in enumerate(near):
+        send(g_send.at[peer], s_all.at[rep, me], gs_sem.at[n], gr_sem.at[me], {"ep": peer})
+    x_recv[me] = x_send[me]
+    s_all[rep, me] = g_send[me]
+
+    def arrived(ref, recv, peer):
+        remote(ref, ref, xs_sem.at[0], recv, {"ep": peer}).wait_recv()
+
+    def spread(ref, send_sem, recv_sem):
+        for n, peer in enumerate(far):
+            send(ref.at[rep], ref.at[rep], send_sem.at[n], recv_sem.at[rep], {"rep": peer})
+        send(ref.at[rep], ref.at[rep], send_sem.at[len(far)], recv_sem.at[rep], {"rep": sibling})
+
+    def swap(ref, send_sem, recv_sem):
+        for n, peer in enumerate(far):
+            arrived(ref.at[peer], recv_sem.at[peer], near[0])
+            send(ref.at[peer], ref.at[peer], send_sem.at[chips + n], recv_sem.at[peer], {"rep": sibling})
+
+    def finish(ref, recv_sem):
+        for k in range(chips):
+            source = ((chip + k) % chips) * 2 + (1 - core)
+            arrived(ref.at[source], recv_sem.at[source], near[0])
+
+    loads[0].wait()
+    loads[1].wait()
+    for peer in near:
+        arrived(x_recv.at[peer], xr_sem.at[peer], peer)
+    x = x_recv[...].reshape(rows, width)
+    pre_gate = dot(x, w_gate[...])
+    pre_up = dot(x, w_up[...])
+    sigma = jax.nn.sigmoid(pre_gate)
+    swish = pre_gate * sigma
+    h_all[rep] = (swish * pre_up).astype(jnp.bfloat16)
+    spread(h_all, hs_sem, hr_sem)
+    loads[2].wait()
+    for peer in near:
+        arrived(s_all.at[rep, peer], gr_sem.at[peer], peer)
+    spread(s_all, ss_sem, sr_sem)
+    d_hidden = dot(s_all[rep].reshape(rows, width), w_down[...], cols_last)
+    d_up = (d_hidden * swish).astype(jnp.bfloat16)
+    d_gate = (d_hidden * pre_up * sigma * (1.0 + pre_gate * (1.0 - sigma))).astype(jnp.bfloat16)
+    d_all[rep, :, :units] = d_gate
+    d_all[rep, :, units:] = d_up
+    spread(d_all, ds_sem, dr_sem)
+    for n, peer in enumerate(others):
+        columns = pl.ds(pl.multiple_of(peer * share, 128), share)
+        send(x_recv.at[:, :, columns], x_own.at[rep], os_sem.at[n], or_sem.at[rep], {"rep": peer})
+    mine = pl.ds(pl.multiple_of(rep * share, 128), share)
+    x_own[rep] = x_recv[:, :, mine]
+    swap(h_all, hs_sem, hr_sem)
+    back = dot(d_gate, w_gate[...], cols_last) + dot(d_up, w_up[...], cols_last)
+    back_send[...] = back.astype(jnp.bfloat16).reshape(owners, CAP, width)
+    for n, peer in enumerate(near):
+        send(back_send.at[peer], ret.at[me], bs_sem.at[n], br_sem.at[me], {"ep": peer})
+    ret[me] = back_send[me]
+    finish(h_all, hr_sem)
+    hidden = h_all[...].reshape(groups * rows, units)
+    hid = dot(hidden, hidden, cols_last)
+    swap(s_all, ss_sem, sr_sem)
+    finish(s_all, sr_sem)
+    scaled = s_all[...].reshape(groups * rows, width)
+    outer = dot(scaled, scaled, cols_last)
+    total = jnp.sum(jnp.sum(outer * hid, axis=0, keepdims=True), axis=1, keepdims=True)
+    total = jnp.maximum(total, 0.0) / (groups * groups)
+    scale = 1.0 / (groups * (jnp.sqrt(total) + norm_eps))
+    power = dot3(split(outer * scale), split(hid * scale))
+    left = s_all[:, :, :, mine].reshape(groups * rows, share).astype(jnp.float32) * scale
+    swap(d_all, ds_sem, dr_sem)
+    size = groups * rows
+    diagonal = lax.broadcasted_iota(jnp.int32, (size, size), 0) == lax.broadcasted_iota(
+        jnp.int32, (size, size), 1
+    )
+    for step in range(ITERS):
+        parts = split(power)
+        poly = coef_cubic * power + coef_quintic * dot3(parts, parts)
+        poly = split(poly + jnp.where(diagonal, coef_linear, 0.0))
+        left = dot3(poly, split(left))
+        if step < ITERS - 1:
+            power = dot3(split(dot3(parts, poly)), poly)
+    left = split(left)
+    down_update[0] = dot(left[0], hidden, rows_first) + dot(left[1], hidden, rows_first)
+    for peer in near:
+        arrived(ret.at[peer], br_sem.at[peer], peer)
+    input_grad[...] = dot(
+        slots[:, :rows].astype(jnp.bfloat16), ret[...].reshape(rows, width)
+    ).astype(jnp.bfloat16)
+    finish(d_all, dr_sem)
+    for peer in others:
+        arrived(x_own.at[peer], or_sem.at[peer], near[0])
+    x_rows = x_own[...].reshape(groups * rows, share)
+    both = dot(x_rows, d_all[...].reshape(groups * rows, 2 * units), rows_first) / groups
+    gate_grad[0] = both[:, :units]
+    up_grad[0] = both[:, units:]
+    for copy in sends:
+        copy.wait_send()
+
+
+def fused(inputs, out_grad, routes, gate_probs, gate_weight, up_weight, down_weight):
+    owners = lax.axis_size("ep")
+    groups = lax.axis_size("rep")
+    tokens, width = inputs.shape
+    units = gate_weight.shape[2]
+    rows = owners * CAP
+    share = width // groups
+    chips = groups // 2
+    half = jnp.bfloat16
+    inside = pl.BlockSpec(memory_space=pltpu.VMEM)
+    outside = pl.BlockSpec(memory_space=pl.ANY)
+    dma = pltpu.SemaphoreType.DMA
+    grads = jax.ShapeDtypeStruct((1, share, units), jnp.float32)
+    return pl.pallas_call(
+        functools.partial(kernel, owners, groups),
+        out_shape=(jax.ShapeDtypeStruct((tokens, width), half), grads, grads, grads),
+        in_specs=[inside] * 4 + [outside] * 3,
+        out_specs=(inside,) * 4,
+        scratch_shapes=[
+            pltpu.VMEM((width, units), half),
+            pltpu.VMEM((width, units), half),
+            pltpu.VMEM((units, width), half),
+            pltpu.VMEM((owners, CAP, width), half),
+            pltpu.VMEM((owners, CAP, width), half),
+            pltpu.VMEM((owners, CAP, width), half),
+            pltpu.VMEM((groups, owners, CAP, width), half),
+            pltpu.VMEM((groups, rows, units), half),
+            pltpu.VMEM((groups, rows, 2 * units), half),
+            pltpu.VMEM((groups, owners, CAP, share), half),
+            pltpu.VMEM((owners, CAP, width), half),
+            pltpu.VMEM((owners, CAP, width), half),
+            dma((3,)),
+        ]
+        + [dma((owners,))] * 6
+        + [dma((groups,))] * 8,
+        compiler_params=pltpu.CompilerParams(
+            collective_id=0, has_side_effects=True, vmem_limit_bytes=52 * 1024 * 1024
+        ),
+    )(inputs, out_grad, routes, gate_probs, gate_weight, up_weight, down_weight)
+
+
 def per_device(inputs, out_grad, routes, gate_probs, gate_weight, up_weight, down_weight):
     owners = lax.axis_size("ep")
     groups = lax.axis_size("rep")
     width = inputs.shape[1]
+    rows = owners * CAP
+    if groups * rows < gate_weight.shape[2] and rows <= 128 and groups % 2 == 0:
+        return fused(inputs, out_grad, routes, gate_probs, gate_weight, up_weight, down_weight)
     dispatch, weight = slot_tables(routes, gate_probs, owners, CAP)
     rows_send = jnp.dot(dispatch, inputs, preferred_element_type=jnp.float32).astype(jnp.bfloat16)
     grad_send = jnp.dot(dispatch, out_grad, preferred_element_type=jnp.float32) * weight[:, None]
     grad_send = grad_send.astype(jnp.bfloat16)
-    rows = owners * CAP
     both_send = jnp.concatenate([rows_send, grad_send], axis=1)
     both_recv = lax.all_to_all(
         both_send.reshape(owners, CAP, 2 * width), "ep", split_axis=0, concat_axis=0, tiled=True

time: 135 us -> 67 us (0.50)
  the two profiles are of different devices: /device:TPU:0 before, /device:TPU:9 now
where the time goes in v2:
time: 67 us; the launch traced here: 66.7 us
  Pallas kernels  57.8 us (86%)
  local copies, waits for them, and re-layouts  8.28 us (12%)
    pallas_call x1, Pallas kernels, fused(): pl.pallas_call(functools.partial(kernel, owners, groups), out_shape=(jax....  57.8 us
    unnamed x14, local copies, waits for them, and re-layouts  8.28 us

profile of v2, /device:TPU:9, one launch (start us, length us, event | category | flops | bytes accessed | tf_op | source)
XLA Modules:
  0.0 66.7 jit_solution(761683636903093182)
XLA Ops:
  0.6 0.8 %copy.11.routes = s32[128,8]{1,0:T(8,128)S(1)} copy(s32[128,8]{0,1:T(8,128)} %param.9) | data formatting | bytes 8192 | tf_op args[2]
  1.4 0.8 %copy.12.gate_probs = f32[128,8]{1,0:T(8,128)S(1)} copy(f32[128,8]{0,1:T(8,128)} %param.10) | data formatting | bytes 8192 | tf_op args[3]
  2.2 0.0 copy-start
  2.2 1.0 %copy-done = bf16[128,2048]{1,0:T(8,128)(2,1)S(1)} copy-done((bf16[128,2048]{1,0:T(8,128)(2,1)S(1)}, bf16[128,2048]{1,0:T(8,128)(2,1)}, u32[]{:S(2)}) %copy-start) | copy-done | bytes 524312
  3.2 0.0 copy-start.1
  3.2 1.0 %copy-done.1 = bf16[128,2048]{1,0:T(8,128)(2,1)S(1)} copy-done((bf16[128,2048]{1,0:T(8,128)(2,1)S(1)}, bf16[128,2048]{1,0:T(8,128)(2,1)}, u32[]{:S(2)}) %copy-start.1) | copy-done | bytes 524312
  4.3 57.8 %shard_map.102 = (bf16[128,2048]{1,0:T(8,128)(2,1)S(1)}, f32[1,256,768]{2,1,0:T(8,128)}, f32[1,256,768]{2,1,0:T(8,128)}, f32[1,256,768]{2,1,0:T(8,128)}) custom-call(bf16[128,2048]{1,0:T(8,128)(2,1)S(1)} %copy-done, bf16[128,2048]{1,0:T(8,128)(2,1)S(1)} %copy-done.1, s32[128,8]{1,0:T(8,128)S(1)} %copy.11.routes, f32[128,8]{1,0:T(8,128)S(1)} %copy.12.gate_probs, ...), custom_call_target="tpu_custom_call" | custom-call | tf_op jit(solution)/shard_map/pallas_call | solution.py:277
  62.1 0.0 copy-start.3
  62.1 0.0 copy-start.2
  62.1 0.8 %copy.17 = bf16[128,2048]{1,0:T(8,128)(2,1)} copy(bf16[128,2048]{1,0:T(8,128)(2,1)S(1)} %get-tuple-element.8) | data formatting | bytes 1048576
  62.9 2.1 %copy.18 = f32[1,256,768]{2,1,0:T(8,128)} copy(f32[1,256,768]{2,1,0:T(8,128)} %get-tuple-element.9) | data formatting | bytes 1572864
  65.0 0.0 copy-done.3
  65.0 0.9 %copy.19 = f32[1,256,768]{2,1,0:T(8,128)} copy(f32[1,256,768]{2,1,0:T(8,128)S(1)} %copy-done.3) | data formatting | bytes 1572864
  65.8 0.0 copy-done.2
  65.8 0.9 %copy.20 = f32[1,256,768]{2,1,0:T(8,128)} copy(f32[1,256,768]{2,1,0:T(8,128)S(1)} %copy-done.2) | data formatting | bytes 1572864
Async XLA Ops:
  2.2 1.0 %copy-start = (bf16[128,2048]{1,0:T(8,128)(2,1)S(1)}, bf16[128,2048]{1,0:T(8,128)(2,1)}, u32[]{:S(2)}) copy-start(bf16[128,2048]{1,0:T(8,128)(2,1)} %inputs.1) | copy-start | bytes 1572868
  3.2 1.0 %copy-start.1 = (bf16[128,2048]{1,0:T(8,128)(2,1)S(1)}, bf16[128,2048]{1,0:T(8,128)(2,1)}, u32[]{:S(2)}) copy-start(bf16[128,2048]{1,0:T(8,128)(2,1)} %out_grad.1) | copy-start | bytes 1572868
  62.1 2.9 %copy-start.3 = (f32[1,256,768]{2,1,0:T(8,128)S(1)}, f32[1,256,768]{2,1,0:T(8,128)}, u32[]{:S(2)}) copy-start(f32[1,256,768]{2,1,0:T(8,128)} %get-tuple-element.10) | copy-start | bytes 2359300
  62.1 3.8 %copy-start.2 = (f32[1,256,768]{2,1,0:T(8,128)S(1)}, f32[1,256,768]{2,1,0:T(8,128)}, u32[]{:S(2)}) copy-start(f32[1,256,768]{2,1,0:T(8,128)} %get-tuple-element.11) | copy-start | bytes 2359300

commit v3 on v2

--- a/solution.py
+++ b/solution.py
@@ -104,9 +104,9 @@
 
 def kernel(
     owners, groups,
-    inputs, out_grad, routes, gate_probs, gate_hbm, up_hbm, down_hbm,
+    inputs_hbm, grad_hbm, routes, gate_probs, gate_hbm, up_hbm, down_hbm,
     input_grad, gate_grad, up_grad, down_update,
-    w_gate, w_up, w_down, x_send, g_send, x_recv, s_all, h_all, d_all, x_own, back_send, ret,
+    inputs, out_grad, w_gate, w_up, w_down, x_send, g_send, x_recv, s_all, h_all, d_all, x_own, back_send, ret,
     w_sem, xs_sem, xr_sem, gs_sem, gr_sem, bs_sem, br_sem,
     os_sem, or_sem, ss_sem, sr_sem, hs_sem, hr_sem, ds_sem, dr_sem,
 ):
@@ -120,38 +120,43 @@
     units = h_all.shape[2]
     rows = owners * CAP
     share = width // groups
-    near = [(me + k) % owners for k in range(1, owners)]
+    if owners == 4:
+        near = [me + 1 - 2 * (me % 2), (me + 2) % 4, 3 - me]
+    else:
+        near = [(me + k) % owners for k in range(1, owners)]
     far = [((chip + k) % chips) * 2 + core for k in range(1, chips)]
     others = [(rep + k) % groups for k in range(1, groups)]
 
-    loads = [
-        pltpu.make_async_copy(src, dst, w_sem.at[n])
-        for n, (src, dst) in enumerate(((gate_hbm.at[0], w_gate), (up_hbm.at[0], w_up), (down_hbm.at[0], w_down)))
-    ]
-    for load in loads:
-        load.start()
     barrier = pltpu.get_barrier_semaphore()
     for peer in near:
         pl.semaphore_signal(barrier, inc=1, device_id={"ep": peer}, device_id_type=pl.DeviceIdType.MESH)
     for peer in others:
         pl.semaphore_signal(barrier, inc=1, device_id={"rep": peer}, device_id_type=pl.DeviceIdType.MESH)
 
-    lane = lax.broadcasted_iota(jnp.int32, (tokens, 128), 1)
-    place = (lane % CAP).astype(jnp.float32)
-    expert = jnp.where(lane < rows, lane // CAP, -1)
-    named = jnp.zeros((tokens, 128), jnp.float32)
-    weight = jnp.zeros((tokens, 128), jnp.float32)
-    for k in range(routes.shape[1]):
-        hit = routes[:, k : k + 1] == expert
+    loads = [
+        pltpu.make_async_copy(src, dst, w_sem.at[n])
+        for n, (src, dst) in enumerate(((gate_hbm.at[0], w_gate), (up_hbm.at[0], w_up), (down_hbm.at[0], w_down),
+        (inputs_hbm, inputs), (grad_hbm, out_grad)))
+    ]
+    for n in (3, 4, 0, 1, 2):
+        loads[n].start()
+    line = lax.broadcasted_iota(jnp.int32, (rows, tokens), 0)
+    place = (line % CAP).astype(jnp.float32)
+    expert = line // CAP
+    named = jnp.zeros((rows, tokens), jnp.float32)
+    weight = jnp.zeros((rows, tokens), jnp.float32)
+    for k in range(routes.shape[0]):
+        hit = routes[k : k + 1, :] == expert
         named = named + jnp.where(hit, 1.0, 0.0)
-        weight = weight + jnp.where(hit, gate_probs[:, k : k + 1], 0.0)
-    earlier = lax.broadcasted_iota(jnp.int32, (tokens, tokens), 1) < lax.broadcasted_iota(
-        jnp.int32, (tokens, tokens), 0
-    )
-    before = dot(jnp.where(earlier, 1.0, 0.0).astype(jnp.bfloat16), named.astype(jnp.bfloat16))
+        weight = weight + jnp.where(hit, gate_probs[k : k + 1, :], 0.0)
+    earlier = lax.broadcasted_iota(jnp.int32, (tokens, tokens), 0) < lax.broadcasted_iota(
+        jnp.int32, (tokens, tokens), 1
+    )
+    before = dot(named.astype(jnp.bfloat16), jnp.where(earlier, 1.0, 0.0).astype(jnp.bfloat16))
     slots = jnp.where(before == place, named, 0.0)
-    dispatch = slots.T[:rows].astype(jnp.bfloat16)
-    weight = jnp.sum((slots * weight).T[:rows], axis=1, keepdims=True)
+    dispatch = slots.astype(jnp.bfloat16)
+    weight = jnp.sum(slots * weight, axis=1, keepdims=True)
+    loads[3].wait()
     x_send[...] = dot(dispatch, inputs[...]).astype(jnp.bfloat16).reshape(owners, CAP, width)
     pl.semaphore_wait(barrier, len(near) + len(others))
     sends = []
@@ -163,6 +168,7 @@
 
     for n, peer in enumerate(near):
         send(x_send.at[peer], x_recv.at[me], xs_sem.at[n], xr_sem.at[me], {"ep": peer})
+    loads[4].wait()
     g_send[...] = (dot(dispatch, out_grad[...]) * weight).astype(jnp.bfloat16).reshape(owners, CAP, width)
     for n, peer in enumerate(near):
         send(g_send.at[peer], s_all.at[rep, me], gs_sem.at[n], gr_sem.at[me], {"ep": peer})
@@ -172,6 +178,14 @@
     def arrived(ref, recv, peer):
         remote(ref, ref, xs_sem.at[0], recv, {"ep": peer}).wait_recv()
 
+    def piece(j):
+        block = s_all.at[rep, j]
+        for n, peer in enumerate(far):
+            send(block, block, ss_sem.at[n, j], sr_sem.at[rep, j], {"rep": peer})
+        send(block, block, ss_sem.at[len(far), j], sr_sem.at[rep, j], {"rep": sibling})
+
+    piece(me)
+
     def spread(ref, send_sem, recv_sem):
         for n, peer in enumerate(far):
             send(ref.at[rep], ref.at[rep], send_sem.at[n], recv_sem.at[rep], {"rep": peer})
@@ -187,10 +201,13 @@
             source = ((chip + k) % chips) * 2 + (1 - core)
             arrived(ref.at[source], recv_sem.at[source], near[0])
 
+    for peer in near:
+        arrived(x_recv.at[peer], xr_sem.at[peer], peer)
+    for n, peer in enumerate(others):
+        columns = pl.ds(pl.multiple_of(peer * share, 128), share)
+        send(x_recv.at[:, :, columns], x_own.at[rep], os_sem.at[n], or_sem.at[rep], {"rep": peer})
     loads[0].wait()
     loads[1].wait()
-    for peer in near:
-        arrived(x_recv.at[peer], xr_sem.at[peer], peer)
     x = x_recv[...].reshape(rows, width)
     pre_gate = dot(x, w_gate[...])
     pre_up = dot(x, w_up[...])
@@ -201,16 +218,12 @@
     loads[2].wait()
     for peer in near:
         arrived(s_all.at[rep, peer], gr_sem.at[peer], peer)
-    spread(s_all, ss_sem, sr_sem)
+        piece(peer)
     d_hidden = dot(s_all[rep].reshape(rows, width), w_down[...], cols_last)
     d_up = (d_hidden * swish).astype(jnp.bfloat16)
     d_gate = (d_hidden * pre_up * sigma * (1.0 + pre_gate * (1.0 - sigma))).astype(jnp.bfloat16)
     d_all[rep, :, :units] = d_gate
     d_all[rep, :, units:] = d_up
-    spread(d_all, ds_sem, dr_sem)
-    for n, peer in enumerate(others):
-        columns = pl.ds(pl.multiple_of(peer * share, 128), share)
-        send(x_recv.at[:, :, columns], x_own.at[rep], os_sem.at[n], or_sem.at[rep], {"rep": peer})
     mine = pl.ds(pl.multiple_of(rep * share, 128), share)
     x_own[rep] = x_recv[:, :, mine]
     swap(h_all, hs_sem, hr_sem)
@@ -222,8 +235,16 @@
     finish(h_all, hr_sem)
     hidden = h_all[...].reshape(groups * rows, units)
     hid = dot(hidden, hidden, cols_last)
-    swap(s_all, ss_sem, sr_sem)
-    finish(s_all, sr_sem)
+    for j in [me] + near:
+        for n, peer in enumerate(far):
+            block = s_all.at[peer, j]
+            arrived(block, sr_sem.at[peer, j], near[0])
+            send(block, block, ss_sem.at[chips + n, j], sr_sem.at[peer, j], {"rep": sibling})
+    spread(d_all, ds_sem, dr_sem)
+    for j in [me] + near:
+        for k in range(chips):
+            source = ((chip + k) % chips) * 2 + (1 - core)
+            arrived(s_all.at[source, j], sr_sem.at[source, j], near[0])
     scaled = s_all[...].reshape(groups * rows, width)
     outer = dot(scaled, scaled, cols_last)
     total = jnp.sum(jnp.sum(outer * hid, axis=0, keepdims=True), axis=1, keepdims=True)
@@ -231,7 +252,6 @@
     scale = 1.0 / (groups * (jnp.sqrt(total) + norm_eps))
     power = dot3(split(outer * scale), split(hid * scale))
     left = s_all[:, :, :, mine].reshape(groups * rows, share).astype(jnp.float32) * scale
-    swap(d_all, ds_sem, dr_sem)
     size = groups * rows
     diagonal = lax.broadcasted_iota(jnp.int32, (size, size), 0) == lax.broadcasted_iota(
         jnp.int32, (size, size), 1
@@ -243,12 +263,14 @@
         left = dot3(poly, split(left))
         if step < ITERS - 1:
             power = dot3(split(dot3(parts, poly)), poly)
+        if step == ITERS - 2:
+            swap(d_all, ds_sem, dr_sem)
     left = split(left)
     down_update[0] = dot(left[0], hidden, rows_first) + dot(left[1], hidden, rows_first)
     for peer in near:
         arrived(ret.at[peer], br_sem.at[peer], peer)
     input_grad[...] = dot(
-        slots[:, :rows].astype(jnp.bfloat16), ret[...].reshape(rows, width)
+        dispatch, ret[...].reshape(rows, width), rows_first
     ).astype(jnp.bfloat16)
     finish(d_all, dr_sem)
     for peer in others:
@@ -277,9 +299,11 @@
     return pl.pallas_call(
         functools.partial(kernel, owners, groups),
         out_shape=(jax.ShapeDtypeStruct((tokens, width), half), grads, grads, grads),
-        in_specs=[inside] * 4 + [outside] * 3,
+        in_specs=[outside] * 2 + [inside] * 2 + [outside] * 3,
         out_specs=(inside,) * 4,
         scratch_shapes=[
+            pltpu.VMEM((tokens, width), half),
+            pltpu.VMEM((tokens, width), half),
             pltpu.VMEM((width, units), half),
             pltpu.VMEM((width, units), half),
             pltpu.VMEM((units, width), half),
@@ -292,14 +316,16 @@
             pltpu.VMEM((groups, owners, CAP, share), half),
             pltpu.VMEM((owners, CAP, width), half),
             pltpu.VMEM((owners, CAP, width), half),
-            dma((3,)),
+            dma((5,)),
         ]
         + [dma((owners,))] * 6
-        + [dma((groups,))] * 8,
+        + [dma((groups,))] * 2
+        + [dma((groups, owners))] * 2
+        + [dma((groups,))] * 4,
         compiler_params=pltpu.CompilerParams(
             collective_id=0, has_side_effects=True, vmem_limit_bytes=52 * 1024 * 1024
         ),
-    )(inputs, out_grad, routes, gate_probs, gate_weight, up_weight, down_weight)
+    )(inputs, out_grad, routes.T, gate_probs.T, gate_weight, up_weight, down_weight)
 
 
 def per_device(inputs, out_grad, routes, gate_probs, gate_weight, up_weight, down_weight):

time: 67 us -> 60.2 us (0.90)
  the two profiles are of different devices: /device:TPU:9 before, /device:TPU:0 now
where the time goes in v3:
time: 60.2 us; the launch traced here: 59.9 us
  Pallas kernels  51.1 us (85%)
  local copies, waits for them, and re-layouts  8.07 us (13%)
  between operations  0.67 us (1%)
    pallas_call x1, Pallas kernels, fused(): pl.pallas_call(functools.partial(kernel, owners, groups), out_shape=(jax....  51.1 us
    unnamed x16, local copies, waits for them, and re-layouts  8.07 us

profile of v3, /device:TPU:0, one launch (start us, length us, event | category | flops | bytes accessed | tf_op | source)
XLA Modules:
  0.0 59.9 jit_solution(11115923815524205941)
XLA Ops:
  0.6 0.0 copy-start
  0.6 1.0 %copy-done = bf16[128,2048]{1,0:T(8,128)(2,1)S(1)} copy-done((bf16[128,2048]{1,0:T(8,128)(2,1)S(1)}, bf16[128,2048]{1,0:T(8,128)(2,1)}, u32[]{:S(2)}) %copy-start) | copy-done | bytes 524312
  1.7 0.0 copy-start.1
  1.7 1.0 %copy-done.1 = bf16[128,2048]{1,0:T(8,128)(2,1)S(1)} copy-done((bf16[128,2048]{1,0:T(8,128)(2,1)S(1)}, bf16[128,2048]{1,0:T(8,128)(2,1)}, u32[]{:S(2)}) %copy-start.1) | copy-done | bytes 524312
  2.7 0.0 copy-start.2
  2.7 0.7 %copy-done.2 = s32[128,8]{0,1:T(8,128)S(1)} copy-done((s32[128,8]{0,1:T(8,128)S(1)}, s32[128,8]{0,1:T(8,128)}, u32[]{:S(2)}) %copy-start.2) | copy-done | bytes 4120
  3.4 0.0 copy-start.3
  3.4 0.7 %copy-done.3 = f32[128,8]{0,1:T(8,128)S(1)} copy-done((f32[128,8]{0,1:T(8,128)S(1)}, f32[128,8]{0,1:T(8,128)}, u32[]{:S(2)}) %copy-start.3) | copy-done | bytes 4120
  4.1 51.1 %shard_map.102 = (bf16[128,2048]{1,0:T(8,128)(2,1)S(1)}, f32[1,256,768]{2,1,0:T(8,128)}, f32[1,256,768]{2,1,0:T(8,128)}, f32[1,256,768]{2,1,0:T(8,128)}) custom-call(bf16[128,2048]{1,0:T(8,128)(2,1)S(1)} %copy-done, bf16[128,2048]{1,0:T(8,128)(2,1)S(1)} %copy-done.1, s32[8,128]{1,0:T(8,128)S(1)} %bitcast.2, f32[8,128]{1,0:T(8,128)S(1)} %bitcast.3, ...), custom_call_target="tpu_custom_call" | custom-call | tf_op jit(solution)/shard_map/pallas_call | solution.py:299
  55.2 0.0 copy-start.5
  55.3 0.0 copy-start.4
  55.3 0.8 %copy.15 = bf16[128,2048]{1,0:T(8,128)(2,1)} copy(bf16[128,2048]{1,0:T(8,128)(2,1)S(1)} %get-tuple-element.8) | data formatting | bytes 1048576
  56.1 2.1 %copy.16 = f32[1,256,768]{2,1,0:T(8,128)} copy(f32[1,256,768]{2,1,0:T(8,128)} %get-tuple-element.9) | data formatting | bytes 1572864
  58.1 0.0 copy-done.5
  58.1 0.9 %copy.17 = f32[1,256,768]{2,1,0:T(8,128)} copy(f32[1,256,768]{2,1,0:T(8,128)S(1)} %copy-done.5) | data formatting | bytes 1572864
  59.0 0.0 copy-done.4
  59.0 0.9 %copy.18 = f32[1,256,768]{2,1,0:T(8,128)} copy(f32[1,256,768]{2,1,0:T(8,128)S(1)} %copy-done.4) | data formatting | bytes 1572864
Async XLA Ops:
  0.6 1.0 %copy-start = (bf16[128,2048]{1,0:T(8,128)(2,1)S(1)}, bf16[128,2048]{1,0:T(8,128)(2,1)}, u32[]{:S(2)}) copy-start(bf16[128,2048]{1,0:T(8,128)(2,1)} %inputs_hbm.1) | copy-start | bytes 1572868
  1.7 1.0 %copy-start.1 = (bf16[128,2048]{1,0:T(8,128)(2,1)S(1)}, bf16[128,2048]{1,0:T(8,128)(2,1)}, u32[]{:S(2)}) copy-start(bf16[128,2048]{1,0:T(8,128)(2,1)} %grad_hbm.1) | copy-start | bytes 1572868
  2.7 0.7 %copy-start.2 = (s32[128,8]{0,1:T(8,128)S(1)}, s32[128,8]{0,1:T(8,128)}, u32[]{:S(2)}) copy-start(s32[128,8]{0,1:T(8,128)} %param.9) | copy-start | bytes 12292
  3.4 0.7 %copy-start.3 = (f32[128,8]{0,1:T(8,128)S(1)}, f32[128,8]{0,1:T(8,128)}, u32[]{:S(2)}) copy-start(f32[128,8]{0,1:T(8,128)} %param.10) | copy-start | bytes 12292
  55.2 2.9 %copy-start.5 = (f32[1,256,768]{2,1,0:T(8,128)S(1)}, f32[1,256,768]{2,1,0:T(8,128)}, u32[]{:S(2)}) copy-start(f32[1,256,768]{2,1,0:T(8,128)} %get-tuple-element.10) | copy-start | bytes 2359300
  55.3 3.8 %copy-start.4 = (f32[1,256,768]{2,1,0:T(8,128)S(1)}, f32[1,256,768]{2,1,0:T(8,128)}, u32[]{:S(2)}) copy-start(f32[1,256,768]{2,1,0:T(8,128)} %get-tuple-element.11) | copy-start | bytes 2359300

commit v4 on v3

--- a/solution.py
+++ b/solution.py
@@ -105,10 +105,10 @@
 def kernel(
     owners, groups,
     inputs_hbm, grad_hbm, routes, gate_probs, gate_hbm, up_hbm, down_hbm,
-    input_grad, gate_grad, up_grad, down_update,
+    slots_out, left_out, h_out, d_out, x_out, ret_out,
     inputs, out_grad, w_gate, w_up, w_down, x_send, g_send, x_recv, s_all, h_all, d_all, x_own, back_send, ret,
     w_sem, xs_sem, xr_sem, gs_sem, gr_sem, bs_sem, br_sem,
-    os_sem, or_sem, ss_sem, sr_sem, hs_sem, hr_sem, ds_sem, dr_sem,
+    o_sem, os_sem, or_sem, ss_sem, sr_sem, hs_sem, hr_sem, ds_sem, dr_sem,
 ):
     me = lax.axis_index("ep")
     rep = lax.axis_index("rep")
@@ -155,6 +155,7 @@
     before = dot(named.astype(jnp.bfloat16), jnp.where(earlier, 1.0, 0.0).astype(jnp.bfloat16))
     slots = jnp.where(before == place, named, 0.0)
     dispatch = slots.astype(jnp.bfloat16)
+    slots_out[...] = dispatch
     weight = jnp.sum(slots * weight, axis=1, keepdims=True)
     loads[3].wait()
     x_send[...] = dot(dispatch, inputs[...]).astype(jnp.bfloat16).reshape(owners, CAP, width)
@@ -233,6 +234,11 @@
         send(back_send.at[peer], ret.at[me], bs_sem.at[n], br_sem.at[me], {"ep": peer})
     ret[me] = back_send[me]
     finish(h_all, hr_sem)
+    stores = [
+        pltpu.make_async_copy(src, dst, o_sem.at[n])
+        for n, (src, dst) in enumerate(((h_all, h_out), (ret, ret_out), (x_own, x_out), (d_all, d_out)))
+    ]
+    stores[0].start()
     hidden = h_all[...].reshape(groups * rows, units)
     hid = dot(hidden, hidden, cols_last)
     for j in [me] + near:
@@ -256,31 +262,42 @@
     diagonal = lax.broadcasted_iota(jnp.int32, (size, size), 0) == lax.broadcasted_iota(
         jnp.int32, (size, size), 1
     )
-    for step in range(ITERS):
+    for step in range(ITERS - 1):
         parts = split(power)
         poly = coef_cubic * power + coef_quintic * dot3(parts, parts)
         poly = split(poly + jnp.where(diagonal, coef_linear, 0.0))
         left = dot3(poly, split(left))
-        if step < ITERS - 1:
-            power = dot3(split(dot3(parts, poly)), poly)
-        if step == ITERS - 2:
-            swap(d_all, ds_sem, dr_sem)
-    left = split(left)
-    down_update[0] = dot(left[0], hidden, rows_first) + dot(left[1], hidden, rows_first)
+        power = dot3(split(dot3(parts, poly)), poly)
+    swap(d_all, ds_sem, dr_sem)
+    parts = split(power)
+    left = coef_linear * left + dot3(
+        parts, split(coef_cubic * left + coef_quintic * dot3(parts, split(left)))
+    )
+    top, rest = split(left)
+    left_out[0] = top
+    left_out[1] = rest
     for peer in near:
         arrived(ret.at[peer], br_sem.at[peer], peer)
-    input_grad[...] = dot(
-        dispatch, ret[...].reshape(rows, width), rows_first
-    ).astype(jnp.bfloat16)
-    finish(d_all, dr_sem)
+    stores[1].start()
     for peer in others:
         arrived(x_own.at[peer], or_sem.at[peer], near[0])
-    x_rows = x_own[...].reshape(groups * rows, share)
-    both = dot(x_rows, d_all[...].reshape(groups * rows, 2 * units), rows_first) / groups
-    gate_grad[0] = both[:, :units]
-    up_grad[0] = both[:, units:]
+    stores[2].start()
+    finish(d_all, dr_sem)
+    stores[3].start()
+    for store in stores:
+        store.wait()
     for copy in sends:
         copy.wait_send()
+
+
+def products(groups, slots, ret, left, x_own, hidden, d_gate, d_up, input_grad, gate_grad, up_grad, down_update):
+    @pl.when(pl.program_id(0) == 0)
+    def _():
+        input_grad[...] = dot(slots[...], ret[...], rows_first).astype(jnp.bfloat16)
+
+    gate_grad[0] = dot(x_own[...], d_gate[...], rows_first) / groups
+    up_grad[0] = dot(x_own[...], d_up[...], rows_first) / groups
+    down_update[0] = dot(left[0], hidden[...], rows_first) + dot(left[1], hidden[...], rows_first)
 
 
 def fused(inputs, out_grad, routes, gate_probs, gate_weight, up_weight, down_weight):
@@ -295,12 +312,13 @@
     inside = pl.BlockSpec(memory_space=pltpu.VMEM)
     outside = pl.BlockSpec(memory_space=pl.ANY)
     dma = pltpu.SemaphoreType.DMA
-    grads = jax.ShapeDtypeStruct((1, share, units), jnp.float32)
-    return pl.pallas_call(
+    shapes = [(rows, tokens), (2, groups * rows, share), (groups, rows, units),
+              (groups, rows, 2 * units), (groups, owners, CAP, share), (owners, CAP, width)]
+    slots, left, h_all, d_all, x_own, ret = pl.pallas_call(
         functools.partial(kernel, owners, groups),
-        out_shape=(jax.ShapeDtypeStruct((tokens, width), half), grads, grads, grads),
+        out_shape=[jax.ShapeDtypeStruct(shape, half) for shape in shapes],
         in_specs=[outside] * 2 + [inside] * 2 + [outside] * 3,
-        out_specs=(inside,) * 4,
+        out_specs=[inside] * 2 + [outside] * 4,
         scratch_shapes=[
             pltpu.VMEM((tokens, width), half),
             pltpu.VMEM((tokens, width), half),
@@ -319,13 +337,37 @@
             dma((5,)),
         ]
         + [dma((owners,))] * 6
+        + [dma((4,))]
         + [dma((groups,))] * 2
         + [dma((groups, owners))] * 2
         + [dma((groups,))] * 4,
         compiler_params=pltpu.CompilerParams(
-            collective_id=0, has_side_effects=True, vmem_limit_bytes=52 * 1024 * 1024
+            collective_id=0, has_side_effects=True, vmem_limit_bytes=62 * 1024 * 1024
         ),
     )(inputs, out_grad, routes.T, gate_probs.T, gate_weight, up_weight, down_weight)
+    total = groups * rows
+    block = 256 if units % 256 == 0 else units
+    steps = units // block
+    d_rows = d_all.reshape(total, 2 * units)
+    fixed = lambda i: (0, 0)
+    return pl.pallas_call(
+        functools.partial(products, groups),
+        grid=(steps,),
+        out_shape=(jax.ShapeDtypeStruct((tokens, width), half),)
+        + (jax.ShapeDtypeStruct((1, share, units), jnp.float32),) * 3,
+        in_specs=[
+            pl.BlockSpec((rows, tokens), fixed),
+            pl.BlockSpec((rows, width), fixed),
+            pl.BlockSpec((2, total, share), lambda i: (0, 0, 0)),
+            pl.BlockSpec((total, share), fixed),
+            pl.BlockSpec((total, block), lambda i: (0, i)),
+            pl.BlockSpec((total, block), lambda i: (0, i)),
+            pl.BlockSpec((total, block), lambda i: (0, i + steps)),
+        ],
+        out_specs=(pl.BlockSpec((tokens, width), fixed),)
+        + (pl.BlockSpec((1, share, block), lambda i: (0, 0, i)),) * 3,
+    )(slots, ret.reshape(rows, width), left, x_own.reshape(total, share),
+      h_all.reshape(total, units), d_rows, d_rows)
 
 
 def per_device(inputs, out_grad, routes, gate_probs, gate_weight, up_weight, down_weight):

time: 60.2 us -> 56.4 us (0.937)
  local copies, waits for them, and re-layouts: 8.07 us -> 0 us
  Pallas kernels: 51.1 us -> 55.5 us
    unnamed x16 -> x0, local copies, waits for them, and re-layouts: 8.07 us -> none
    pallas_call x1 -> x2, Pallas kernels: 51.1 us -> 55.5 us  [the longest x1 50.5 us: fused(): pl.pallas_call(functools.partial(kernel, owners, groups), out_shape=[jax....]
where the time goes in v4:
time: 56.4 us; the launch traced here: 56.2 us
  Pallas kernels  55.5 us (98%)
  between operations  0.64 us (1%)
    pallas_call x1, Pallas kernels, fused(): pl.pallas_call(functools.partial(kernel, owners, groups), out_shape=[jax....  50.5 us
    pallas_call x1, Pallas kernels, fused(): pl.pallas_call(functools.partial(products, groups), grid=(steps,), out_sh...  5.05 us

profile of v4, /device:TPU:0, one launch (start us, length us, event | category | flops | bytes accessed | tf_op | source)
XLA Modules:
  0.0 56.2 jit_solution(12981198176857975399)
XLA Ops:
  0.6 50.5 %shard_map.102 = (bf16[64,128]{1,0:T(8,128)(2,1)}, bf16[2,512,256]{2,1,0:T(8,128)(2,1)}, bf16[8,64,768]{2,1,0:T(8,128)(2,1)}, bf16[8,64,1536]{2,1,0:T(8,128)(2,1...) custom-call(bf16[128,2048]{1,0:T(8,128)(2,1)} %inputs_hbm.1, bf16[128,2048]{1,0:T(8,128)(2,1)} %grad_hbm.1, ...), custom_call_target="tpu_custom_call" | custom-call | tf_op jit(solution)/shard_map/pallas_call | solution.py:317
  51.1 5.0 %shard_map.103 = (bf16[128,2048]{1,0:T(8,128)(2,1)}, f32[1,256,768]{2,1,0:T(8,128)}, f32[1,256,768]{2,1,0:T(8,128)}, f32[1,256,768]{2,1,0:T(8,128)}) custom-call(bf16[64,128]{1,0:T(8,128)(2,1)} %get-tuple-element.10.slots, bf16[64,2048]{1,0:T(8,128)(2,1)} %bitcast.10, bf16[2,512,256]{2,1,0:T(8,128)(2,1)} %get-tuple-element.12.left, ...), custom_call_target="tpu_custom_call" | custom-call | tf_op jit(solution)/shard_map/pallas_call | solution.py:353

commit v5 on v4

--- a/solution.py
+++ b/solution.py
@@ -92,7 +92,9 @@
 
 
 def dot3(left, right):
-    return dot(left[0], right[0]) + (dot(left[0], right[1]) + dot(left[1], right[0]))
+    wide = jnp.concatenate([left[0], left[0], left[1]], axis=1)
+    tall = jnp.concatenate([right[0], right[1], right[0]], axis=0)
+    return dot(wide, tall)
 
 
 def remote(src, dst, send, recv, device):

time: 56.4 us -> 52.2 us (0.926)
  Pallas kernels: 55.5 us -> 51.4 us
    pallas_call x1, Pallas kernels: 50.5 us -> 46.3 us  [fused(): pl.pallas_call(functools.partial(kernel, owners, groups), out_shape=[jax....]
where the time goes in v5:
time: 52.2 us; the launch traced here: 52 us
  Pallas kernels  51.4 us (98%)
  between operations  0.64 us (1%)
    pallas_call x1, Pallas kernels, fused(): pl.pallas_call(functools.partial(kernel, owners, groups), out_shape=[jax....  46.3 us
    pallas_call x1, Pallas kernels, fused(): pl.pallas_call(functools.partial(products, groups), grid=(steps,), out_sh...  5.05 us

profile of v5, /device:TPU:0, one launch (start us, length us, event | category | flops | bytes accessed | tf_op | source)
XLA Modules:
  0.0 52.0 jit_solution(186022944716573283)
XLA Ops:
  0.6 46.3 %shard_map.102 = (bf16[64,128]{1,0:T(8,128)(2,1)}, bf16[2,512,256]{2,1,0:T(8,128)(2,1)}, bf16[8,64,768]{2,1,0:T(8,128)(2,1)}, bf16[8,64,1536]{2,1,0:T(8,128)(2,1...) custom-call(bf16[128,2048]{1,0:T(8,128)(2,1)} %inputs_hbm.1, bf16[128,2048]{1,0:T(8,128)(2,1)} %grad_hbm.1, ...), custom_call_target="tpu_custom_call" | custom-call | tf_op jit(solution)/shard_map/pallas_call | solution.py:319
  47.0 5.0 %shard_map.103 = (bf16[128,2048]{1,0:T(8,128)(2,1)}, f32[1,256,768]{2,1,0:T(8,128)}, f32[1,256,768]{2,1,0:T(8,128)}, f32[1,256,768]{2,1,0:T(8,128)}) custom-call(bf16[64,128]{1,0:T(8,128)(2,1)} %get-tuple-element.10.slots, bf16[64,2048]{1,0:T(8,128)(2,1)} %bitcast.10, bf16[2,512,256]{2,1,0:T(8,128)(2,1)} %get-tuple-element.12.left, ...), custom_call_target="tpu_custom_call" | custom-call | tf_op jit(solution)/shard_map/pallas_call | solution.py:355
